TPU v7x, 32 devices: a whole 2x2x4 slice. The times are simulated.
32 devices in a mesh: ctx: 8 (over z, core), head: 4 (over y, x).
Axes of the slice: x: 2, y: 2, z: 4, core: 2. Of those that a mesh axis runs over, the one named last changes fastest.
Arguments:
- queries: bfloat16 [2048, 2048], P('ctx', 'head'), may hold values from -1.1953125 to 1.1953125
- keys: bfloat16 [2048, 2048], P('ctx', 'head'), may hold values from -1.1953125 to 1.1953125
- values: bfloat16 [2048, 2048], P('ctx', 'head'), may hold values from -6 to 6
- log_decay: float32 [2048, 16], P('ctx', 'head'), may hold values from -3 to 0, as said below
- gain: float32 [2048], P('head'), may hold values from 0.1 to 1.9
- grad_normed: bfloat16 [2048, 2048], P('ctx', 'head'), may hold values from -6 to 6
Outputs:
- grad_query: bfloat16 [2048, 2048], P('ctx', 'head')
- grad_key: bfloat16 [2048, 2048], P('ctx', 'head')
- grad_value: bfloat16 [2048, 2048], P('ctx', 'head')
Inputs may be any that keep to these rules, and one draw needn't show every extreme that they name: `log_decay`: negative everywhere.
All inputs are finite; a program needn't handle non-finite values.
Results may differ from a plain program's by a relative error of at most 0.0051.
Values sent between devices are 32-bit elements; how exact they have to be, the bound alone decides.
A program may use at most 64 MiB of HBM per device.

v0:
```python
import jax
import jax.numpy as jnp
from jax import lax
from jax.sharding import PartitionSpec as P


def prefix(part, axis, combine, identity, reverse):
    count = lax.axis_size(axis)
    place = lax.axis_index(axis)
    ahead = count - 1 - place if reverse else place
    gathered = jax.tree.map(lambda a: lax.all_gather(a, axis), part)
    state = jax.tree.map(lambda a, e: jnp.zeros_like(a) + jnp.asarray(e, a.dtype), part, identity)

    def one(hop, state):
        source = count - 1 - hop if reverse else hop
        return combine(
            state, jax.tree.map(lambda a: lax.dynamic_index_in_dim(a, source, 0, False), gathered)
        )

    return lax.fori_loop(0, ahead, one, state)


def block_decay(logd):
    cum = jnp.cumsum(logd, axis=0)
    last = cum[-1]
    trans = cum.T
    diff = trans[:, :, None] - trans[:, None, :]
    count = logd.shape[0]
    lower = jnp.arange(count)[:, None] >= jnp.arange(count)[None, :]
    decay = jnp.where(lower[None], jnp.exp(jnp.minimum(diff, 0.0)), 0.0)
    return (cum, last, decay)


def combine_states(earlier, later):
    return (earlier[0] + later[0], jnp.exp(later[0])[:, None, None] * earlier[1] + later[1])


def on_device(queries, keys, values, log_decay, gain, grad_normed):
    tok_rows = queries.shape[0]
    heads_here = log_decay.shape[1]
    head_size = queries.shape[1] // heads_here
    feats_all = heads_here * head_size * lax.axis_size("head")
    highest = lax.Precision.HIGHEST
    q_in = queries.reshape(tok_rows, heads_here, head_size)
    k_in = keys.reshape(tok_rows, heads_here, head_size)
    v_in = values.reshape(tok_rows, heads_here, head_size)
    dy_in = grad_normed.reshape(tok_rows, heads_here, head_size).astype(jnp.float32)
    gain3 = gain.reshape(heads_here, head_size)
    cum, last, decay = block_decay(log_decay)
    tail = jnp.exp(last[None, :] - cum)[:, :, None]
    lead = jnp.exp(cum)[:, :, None]
    k32 = k_in.astype(jnp.float32)
    v32 = v_in.astype(jnp.float32)
    q32 = q_in.astype(jnp.float32)
    own_state = jnp.einsum("thi,thj->hij", k32 * tail, v32, precision=highest)
    identity = (jnp.zeros_like(last), jnp.zeros_like(own_state))
    state_in = prefix((last, own_state), "ctx", combine_states, identity, False)[1]
    scores = jnp.einsum("thd,shd->hts", q_in, k_in, preferred_element_type=jnp.float32)
    fwd_w = (scores * decay).astype(jnp.bfloat16)
    attn = jnp.einsum("hts,shd->thd", fwd_w, v_in, preferred_element_type=jnp.float32)
    attn = attn + lead * jnp.einsum("thi,hij->thj", q32, state_in, precision=highest)
    local_sq = jnp.sum(attn * attn, axis=(1, 2))
    local_cross = jnp.sum(gain3[None] * dy_in * attn, axis=(1, 2))
    sumsq, cross = lax.psum((local_sq, local_cross), "head")
    rinv = 1.0 / jnp.sqrt(sumsq / feats_all + 1e-06)
    grad_out = (
        gain3[None] * dy_in * rinv[:, None, None]
        - attn * (cross * rinv**3 / feats_all)[:, None, None]
    )
    grad_out = grad_out.astype(jnp.bfloat16)
    go32 = grad_out.astype(jnp.float32)
    own_grad = jnp.einsum("thi,thj->hij", q32 * lead, go32, precision=highest)
    state_grad = prefix((last, own_grad), "ctx", combine_states, identity, True)[1]
    bwd_w = (
        jnp.einsum("thd,shd->hts", grad_out, v_in, preferred_element_type=jnp.float32) * decay
    ).astype(jnp.bfloat16)
    grad_q = jnp.einsum("hts,shd->thd", bwd_w, k_in, preferred_element_type=jnp.float32)
    grad_q = grad_q + lead * jnp.einsum("thj,hij->thi", go32, state_in, precision=highest)
    grad_k = jnp.einsum("hts,thd->shd", bwd_w, q_in, preferred_element_type=jnp.float32)
    grad_k = grad_k + tail * jnp.einsum("thj,hij->thi", v32, state_grad, precision=highest)
    grad_v = jnp.einsum("hts,thd->shd", fwd_w, grad_out, preferred_element_type=jnp.float32)
    grad_v = grad_v + tail * jnp.einsum("thi,hij->thj", k32, state_grad, precision=highest)
    flat = (tok_rows, heads_here * head_size)
    return (
        grad_q.astype(jnp.bfloat16).reshape(flat),
        grad_k.astype(jnp.bfloat16).reshape(flat),
        grad_v.astype(jnp.bfloat16).reshape(flat),
    )


def solution(mesh):
    in_specs = (
        P("ctx", "head"),
        P("ctx", "head"),
        P("ctx", "head"),
        P("ctx", "head"),
        P("head"),
        P("ctx", "head"),
    )
    out_specs = (P("ctx", "head"), P("ctx", "head"), P("ctx", "head"))
    return jax.shard_map(
        on_device, mesh=mesh, in_specs=in_specs, out_specs=out_specs, check_vma=False
    )
```

profile of v0, /device:TPU:1, one launch (start us, length us, event | category | flops | bytes accessed | tf_op | source)
XLA Modules:
  0.0 105.1 jit_solution(3692258656550241132)
XLA Ops:
  7.2 0.7 reshape.92
  8.0 1.2 %reduce-window.6 = f32[4,2,128]{2,1,0:T(2,128)S(1)} reduce-window(f32[4,2,128]{2,1,0:T(2,128)S(1)} %reshape.92, f32[]{:T(128)} %constant.65.clone.1), window={size=1x1x128 pad=0_0x0_0x127_0}, to_apply=%region_0.0 | reduce-window | flops 130048 | bytes 8196 | tf_op jit(solution)/shard_map/reduce-window
  9.8 1.1 %copy.89 = bf16[256,512]{0,1:T(8,128)(2,1)S(1)} copy(bf16[256,512]{1,0:T(8,128)(2,1)} %param.11) | data formatting | bytes 524288 | tf_op args[1]
  11.0 1.1 %fusion.16 = f32[4,128,128]{2,1,0:T(8,128)} fusion(bf16[256,4,128]{0,2,1:T(8,128)(2,1)S(1)} %bitcast.125, f32[256,4]{0,1:T(4,128)S(1)} %get-tuple-element.210, bf16[256,512]{1,0:T(8,128)(2,1)S(1)} %copy-done), kind=kOutput, calls=%fused_computation.34 | convolution fusion | flops 201588736 | bytes 790528 | tf_op jit(solution)/shard_map/thi,thj->hij/dot_general | solution.py:55
  12.1 13.2 %all-gather.2 = f32[8,1,4]{2,1,0:T(1,128)S(1)} all-gather(f32[1,1,4]{2,1,0:T(1,128)S(1)} %bitcast.144), channel_id=1, replica_groups=mesh['ctx'=8,'head'=4] {'ctx'}, dimensions={0}, use_global_device_ids=true | all-gather | bytes 144 | tf_op jit(solution)/shard_map/all_gather | solution.py:11
  25.5 1.1 %copy.88 = bf16[256,512]{0,1:T(8,128)(2,1)S(1)} copy(bf16[256,512]{1,0:T(8,128)(2,1)} %param.10) | data formatting | bytes 524288 | tf_op args[0]
  27.6 16.2 %all-gather.6.cloned.1.call-done = f32[32,128,128]{2,1,0:T(8,128)} async-done(((f32[4,128,128]{2,1,0:T(8,128)}), f32[32,128,128]{2,1,0:T(8,128)}) %all-gather.6.cloned.1.call-update) | async-done | bytes 2097168 | tf_op jit(solution)/shard_map/all_gather | solution.py:11
  43.9 1.1 %while.26 = (s32[]{:T(128)}, f32[4,128,128]{2,1,0:T(8,128)S(1)}, s32[]{:T(128)}, f32[8,4]{1,0:T(8,128)S(1)}, f32[8,4,128,128]{3,2,1,0:T(8,128)}, /*index=5*/s32[]{:T(128)}, s32[]{:T(128)}, s32[]{:T(128)}) while((s32[]{:T(128)}, f32[4,128,128]{2,1,0:T(8,128)S(1)}, s32[]{:T(128)}, f32[8,4]{1,0:T(8,128)S(1)}, f32[8,4,128,128]{3,2,1,0:T(8,128)}, ...), condition=%wide.region_3.4_spmd, body=%wide.region_2.3_spmd.sunk | while | flops 131077 | bytes 786615 | solution.py:20
  43.9 1.1 %bitcast_add_fusion.4 = f32[4,128,128]{2,1,0:T(8,128)S(1)} fusion(f32[8,4,128,128]{3,2,1,0:T(8,128)} %get-tuple-element.300, s32[]{:T(128)S(6)} %select_n.29, f32[4,128,128]{2,1,0:T(8,128)S(1)} %get-tuple-element.289, f32[4]{0:T(128)S(1)} %exponential_bitcast_fusion.4), kind=kLoop, calls=%fused_computation.clone.1 | loop fusion | flops 131072 | bytes 786452 | tf_op jit(solution)/shard_map/while/body/add | solution.py:35
  45.0 0.5 multiply_reduce_fusion.1
  45.5 7.8 %all-reduce = (f32[256]{0:T(256)S(1)}, f32[256]{0:T(256)S(1)}) all-reduce(f32[256]{0:T(256)S(1)} %get-tuple-element.186, f32[256]{0:T(256)S(1)} %get-tuple-element.185), channel_id=1, replica_groups=mesh['ctx'=8,'head'=4] {'head'}, use_global_device_ids=true, to_apply=%region_7.8 | all-reduce | flops 512 | bytes 4096 | tf_op jit(solution)/shard_map/psum | solution.py:64
  53.5 1.1 %fusion.13 = f32[4,128,128]{2,1,0:T(8,128)} fusion(bf16[256,4,128]{0,2,1:T(8,128)(2,1)S(1)} %subtract_convert_fusion, bf16[256,4,128]{0,2,1:T(8,128)(2,1)S(1)} %bitcast.131, f32[256,4]{0,1:T(4,128)S(1)} %get-tuple-element.209), kind=kOutput, calls=%fused_computation.28 | convolution fusion | flops 201588736 | bytes 790528 | tf_op jit(solution)/shard_map/thi,thj->hij/dot_general | solution.py:72
  54.6 0.4 fusion.1
  55.8 0.8 copy.108
  57.1 32.0 %all-gather.8.cloned.1.call-done = f32[32,128,128]{2,1,0:T(8,128)} async-done(((f32[4,128,128]{2,1,0:T(8,128)}), f32[32,128,128]{2,1,0:T(8,128)}) %all-gather.8.cloned.1.call-update) | async-done | bytes 2097168 | tf_op jit(solution)/shard_map/all_gather | solution.py:11
  89.1 6.6 %while.27 = (s32[]{:T(128)}, f32[4,128,128]{2,1,0:T(8,128)S(1)}, s32[]{:T(128)}, f32[8,4]{1,0:T(8,128)S(1)}, f32[8,4,128,128]{3,2,1,0:T(8,128)}, /*index=5*/s32[]{:T(128)}, s32[]{:T(128)}, s32[]{:T(128)}, s32[]{:T(128)}) while((s32[]{:T(128)}, f32[4,128,128]{2,1,0:T(8,128)S(1)}, s32[]{:T(128)}, f32[8,4]{1,0:T(8,128)S(1)}, ...), condition=%wide.region_9.10_spmd, body=%wide.region_8.9_spmd.sunk | while | flops 131078 | bytes 786635 | solution.py:20
  89.1 1.1 %bitcast_add_fusion.5 = f32[4,128,128]{2,1,0:T(8,128)S(1)} fusion(f32[8,4,128,128]{3,2,1,0:T(8,128)} %get-tuple-element.326, s32[]{:T(128)S(6)} %select_n.30, f32[4,128,128]{2,1,0:T(8,128)S(1)} %get-tuple-element.314, f32[4]{0:T(128)S(1)} %exponential_bitcast_fusion.5), kind=kLoop, calls=%fused_computation.2.clone.1 | loop fusion | flops 131072 | bytes 786452 | tf_op jit(solution)/shard_map/while/body/add | solution.py:35
  90.2 1.1 %bitcast_add_fusion.5 = f32[4,128,128]{2,1,0:T(8,128)S(1)} fusion(f32[8,4,128,128]{3,2,1,0:T(8,128)} %get-tuple-element.326, s32[]{:T(128)S(6)} %select_n.30, f32[4,128,128]{2,1,0:T(8,128)S(1)} %get-tuple-element.314, f32[4]{0:T(128)S(1)} %exponential_bitcast_fusion.5), kind=kLoop, calls=%fused_computation.2.clone.1 | loop fusion | flops 131072 | bytes 786452 | tf_op jit(solution)/shard_map/while/body/add | solution.py:35
  91.3 1.1 %bitcast_add_fusion.5 = f32[4,128,128]{2,1,0:T(8,128)S(1)} fusion(f32[8,4,128,128]{3,2,1,0:T(8,128)} %get-tuple-element.326, s32[]{:T(128)S(6)} %select_n.30, f32[4,128,128]{2,1,0:T(8,128)S(1)} %get-tuple-element.314, f32[4]{0:T(128)S(1)} %exponential_bitcast_fusion.5), kind=kLoop, calls=%fused_computation.2.clone.1 | loop fusion | flops 131072 | bytes 786452 | tf_op jit(solution)/shard_map/while/body/add | solution.py:35
  92.4 1.1 %bitcast_add_fusion.5 = f32[4,128,128]{2,1,0:T(8,128)S(1)} fusion(f32[8,4,128,128]{3,2,1,0:T(8,128)} %get-tuple-element.326, s32[]{:T(128)S(6)} %select_n.30, f32[4,128,128]{2,1,0:T(8,128)S(1)} %get-tuple-element.314, f32[4]{0:T(128)S(1)} %exponential_bitcast_fusion.5), kind=kLoop, calls=%fused_computation.2.clone.1 | loop fusion | flops 131072 | bytes 786452 | tf_op jit(solution)/shard_map/while/body/add | solution.py:35
  93.5 1.1 %bitcast_add_fusion.5 = f32[4,128,128]{2,1,0:T(8,128)S(1)} fusion(f32[8,4,128,128]{3,2,1,0:T(8,128)} %get-tuple-element.326, s32[]{:T(128)S(6)} %select_n.30, f32[4,128,128]{2,1,0:T(8,128)S(1)} %get-tuple-element.314, f32[4]{0:T(128)S(1)} %exponential_bitcast_fusion.5), kind=kLoop, calls=%fused_computation.2.clone.1 | loop fusion | flops 131072 | bytes 786452 | tf_op jit(solution)/shard_map/while/body/add | solution.py:35
  94.6 1.1 %bitcast_add_fusion.5 = f32[4,128,128]{2,1,0:T(8,128)S(1)} fusion(f32[8,4,128,128]{3,2,1,0:T(8,128)} %get-tuple-element.326, s32[]{:T(128)S(6)} %select_n.30, f32[4,128,128]{2,1,0:T(8,128)S(1)} %get-tuple-element.314, f32[4]{0:T(128)S(1)} %exponential_bitcast_fusion.5), kind=kLoop, calls=%fused_computation.2.clone.1 | loop fusion | flops 131072 | bytes 786452 | tf_op jit(solution)/shard_map/while/body/add | solution.py:35
  96.1 0.8 copy.110
  97.4 0.8 copy.109
  (42 shorter events, 4.1 us)
Async XLA Ops:
  7.2 3.8 %copy-start = (bf16[256,512]{1,0:T(8,128)(2,1)S(1)}, bf16[256,512]{1,0:T(8,128)(2,1)}, u32[]{:S(2)}) copy-start(bf16[256,512]{1,0:T(8,128)(2,1)} %param.12) | copy-start | bytes 786436
  7.2 19.4 %copy-start.1 = (bf16[256,512]{1,0:T(8,128)(2,1)S(1)}, bf16[256,512]{1,0:T(8,128)(2,1)}, u32[]{:S(2)}) copy-start(bf16[256,512]{1,0:T(8,128)(2,1)} %param.15) | copy-start | bytes 786436
  7.2 36.6 %all-gather.6.cloned.1.call-start = ((), (), s32[]{:S(2)}) async-start(), calls=%async_computation | async-start | bytes 2359296 | tf_op jit(solution)/shard_map/all_gather | solution.py:11
  12.1 77.0 %all-gather.8.cloned.1.call-start = ((), (), s32[]{:S(2)}) async-start(), calls=%async_computation.1 | async-start | bytes 2359296 | tf_op jit(solution)/shard_map/all_gather | solution.py:11
  43.8 1.1 %copy-start.2 = (f32[512]{0:T(512)S(1)}, f32[512]{0:T(512)}, u32[]{:S(2)}) copy-start(f32[512]{0:T(512)} %param.14) | copy-start | bytes 6148
Sparse Core Ops, SparseCore 0:
  12.2 31.5 all-gather.5
  54.8 34.2 all-gather.7
where the time goes:
time: 107 us; the launch traced here: 105 us
  waiting for transfers between devices  48.3 us (45%)
  blocking collectives  21.1 us (20%)
  between operations  14.2 us (13%)
  other arithmetic  9 us (8%)
  local copies, waits for them, and re-layouts  6.34 us (6%)
  matrix products  5.88 us (5%)
    all_gather x2, waiting for transfers between devices, prefix(): gathered = jax.tree.map(lambda a: lax.all_gather(a, axis), part)  48.2 us
    all_gather x1, blocking collectives, prefix(): gathered = jax.tree.map(lambda a: lax.all_gather(a, axis), part)  13.2 us
    psum x1, blocking collectives, on_device(): sumsq, cross = lax.psum((local_sq, local_cross), 'head')  7.83 us
    add x7, other arithmetic, combine_states(): jnp.exp(later[0])[:, None, None] * earlier[1] + later[1]  7.43 us
    unnamed x12, local copies, waits for them, and re-layouts  4.73 us
  transfers between devices with their start and end apart: 2, of which 2 were waited for; matrix products, arithmetic and copies ran while one was open for 4% of the time, Pallas kernels for 0%

commit v1 on v0

v1 whole, which is shorter than its diff:
```python
import functools

import jax
import jax.numpy as jnp
from jax import lax
from jax.experimental import pallas as pl
from jax.experimental.pallas import tpu as pltpu
from jax.sharding import PartitionSpec as P

F32 = jnp.float32
BF16 = jnp.bfloat16
MESH = pl.DeviceIdType.MESH


def mm(a, b, ca=1, cb=0):
    return lax.dot_general(a, b, (((ca,), (cb,)), ((), ())), preferred_element_type=F32)


def kernel(
    nz, nh, feats_all,
    q, k, v, ld, gain, dy,
    gq, gk, gv,
    own_s, sib_s, state, pass_s, own_x, sib_x, sgrad, pass_x, red_tx, red_rx,
    attn, go, fwd_w, decay, part_k, part_v,
    s_tx, s_rx, e_tx, e_rx, c_tx, c_rx, r_tx, r_rx, x_tx, x_rx, f_tx, f_rx, d_tx, d_rx,
):
    toks = q.shape[0]
    heads = ld.shape[1]
    hd = q.shape[1] // heads
    half = heads // 2
    me = lax.axis_index("ctx")
    grp = lax.axis_index("head")
    z = me // 2
    c = me % 2
    sib = me + 1 - 2 * c
    first = c == 0
    has_prev = z > 0
    has_next = z < nz - 1

    def cols(h):
        return slice(h * hd, (h + 1) * hd)

    def copy(src, dst, tx, rx, where):
        return pltpu.make_async_remote_copy(
            src_ref=src, dst_ref=dst, send_sem=tx, recv_sem=rx,
            device_id=where, device_id_type=MESH,
        )

    barrier = pltpu.get_barrier_semaphore()
    pl.semaphore_signal(barrier, inc=1, device_id={"ctx": sib}, device_id_type=MESH)
    for step in (2, 2 * nz - 2):
        pl.semaphore_signal(
            barrier, inc=1, device_id={"ctx": lax.rem(me + step, 2 * nz)}, device_id_type=MESH
        )
    for d in range(1, nh):
        pl.semaphore_signal(
            barrier, inc=1, device_id={"head": lax.rem(grp + d, nh)}, device_id_type=MESH
        )

    row = lax.broadcasted_iota(jnp.int32, (toks, toks), 0)
    col = lax.broadcasted_iota(jnp.int32, (toks, toks), 1)
    lower = row >= col
    tri = jnp.where(lower, 1.0, 0.0).astype(BF16)
    lane = lax.broadcasted_iota(jnp.int32, (toks, 128), 1)
    logd = jnp.zeros((toks, 128), F32)
    for h in range(heads):
        logd = jnp.where(lane == h, ld[:, h : h + 1], logd)
    high = logd.astype(BF16)
    rest = logd - high.astype(F32)
    mid = rest.astype(BF16)
    low = (rest - mid.astype(F32)).astype(BF16)
    cum = mm(tri, high) + mm(tri, mid) + mm(tri, low)
    last = cum[toks - 1 : toks, :]
    lead_all = jnp.exp(cum)
    tail_all = jnp.exp(last - cum)
    cum_t = cum.T

    for h in range(heads):
        kt = (k[:, cols(h)].astype(F32) * tail_all[:, h : h + 1]).astype(BF16)
        own_s[h, :hd, :] = mm(kt, v[:, cols(h)], 0, 0)
        own_s[h, hd:, :] = jnp.broadcast_to(last[:, h : h + 1], (8, hd))

    pl.semaphore_wait(barrier, 2 + nh)

    def swap(src, dst, tx, rx, h):
        return copy(src.at[h], dst.at[h], tx.at[h], rx.at[h], {"ctx": sib})

    for h in range(heads):
        swap(own_s, sib_s, s_tx, s_rx, h).start()

    @pl.when(jnp.logical_not(has_prev))
    def _():
        state[...] = jnp.zeros_like(state)

    @pl.when(jnp.logical_not(has_next))
    def _():
        sgrad[...] = jnp.zeros_like(sgrad)

    def local(h):
        diff = cum[:, h : h + 1] - cum_t[h : h + 1, :]
        dec = jnp.where(lower, jnp.exp(jnp.minimum(diff, 0.0)), 0.0)
        decay[h] = dec
        w = (mm(q[:, cols(h)], k[:, cols(h)], 1, 1) * dec).astype(BF16)
        fwd_w[h] = w
        attn[:, cols(h)] = mm(w, v[:, cols(h)])

    for h in range(half):
        local(h)
    for h in range(heads):
        swap(own_s, sib_s, s_tx, s_rx, h).wait_recv()

    def pick(own, other, h):
        a = own[h, :hd, :]
        b = other[h, :hd, :]
        return jnp.where(first, a, b), jnp.where(first, b, a)

    def logs(h):
        a = own_s[h, hd : hd + 1, :]
        b = sib_s[h, hd : hd + 1, :]
        return jnp.where(first, a, b), jnp.where(first, b, a)

    def hop(buf, dst, tx, rx, j, step):
        return copy(buf.at[j], dst.at[half * c + j], tx.at[j], rx.at[j], {"ctx": me + step})

    def give(buf, tx, rx, j):
        h = half * c + j
        return copy(buf.at[h], buf.at[h], tx.at[j], rx.at[j], {"ctx": sib})

    def take(buf, tx, rx, j):
        h = half * (1 - c) + j
        return copy(buf.at[h], buf.at[h], tx.at[j], rx.at[j], {"ctx": sib})

    for j in range(half):
        h = half * c + j
        s0, s1 = pick(own_s, sib_s, h)
        l0, l1 = logs(h)
        pass_s[j] = jnp.exp(l1) * s0 + s1

        @pl.when(jnp.logical_not(has_prev) & has_next)
        def _():
            hop(pass_s, state, e_tx, e_rx, j, 2).start()

    for h in range(half, heads):
        local(h)

    @pl.when(has_prev)
    def _():
        for j in range(half):
            h = half * c + j
            hop(pass_s, state, e_tx, e_rx, j, 2).wait_recv()
            give(state, c_tx, c_rx, j).start()

            @pl.when(has_next)
            def _():
                l0, l1 = logs(h)
                pass_s[j] = jnp.exp(l0 + l1) * state[h] + pass_s[j]
                hop(pass_s, state, e_tx, e_rx, j, 2).start()

        for j in range(half):
            take(state, c_tx, c_rx, j).wait_recv()

    sq = jnp.zeros((toks, hd), F32)
    cr = jnp.zeros((toks, hd), F32)
    s_in = []
    for h in range(heads):
        l_sib = sib_s[h, hd : hd + 1, :]
        e = state[h]
        e = jnp.where(first, e, jnp.exp(l_sib) * e + sib_s[h, :hd, :])
        e = e.astype(BF16)
        s_in.append(e)
        a = attn[:, cols(h)] + lead_all[:, h : h + 1] * mm(q[:, cols(h)], e)
        attn[:, cols(h)] = a
        sq = sq + a * a
        cr = cr + gain[:, cols(h)] * dy[:, cols(h)].astype(F32) * a
    sq = jnp.sum(sq, axis=1, keepdims=True)
    cr = jnp.sum(cr, axis=1, keepdims=True)
    both = jnp.where(lane == 0, sq, jnp.where(lane == 1, cr, 0.0)).T
    red_tx[...] = both[:8, :]

    def spread(d):
        return copy(
            red_tx, red_rx.at[d - 1], r_tx.at[d - 1], r_rx.at[d - 1],
            {"head": lax.rem(grp + d, nh)},
        )

    for d in range(1, nh):
        spread(d).start()
    total = red_tx[...]
    for d in range(1, nh):
        spread(d).wait_recv()
        total = total + red_rx[d - 1]
    rinv = 1.0 / jnp.sqrt(total[0:1, :] / feats_all + 1e-06)
    coef = total[1:2, :] * (rinv * rinv * rinv) / feats_all
    sub = lax.broadcasted_iota(jnp.int32, (128, toks), 0)
    scal = jnp.where(sub == 0, rinv, jnp.where(sub == 1, coef, 0.0)).T
    rinv_c = scal[:, 0:1]
    coef_c = scal[:, 1:2]

    for h in range(heads):
        g = gain[:, cols(h)] * dy[:, cols(h)].astype(F32) * rinv_c - attn[:, cols(h)] * coef_c
        g = g.astype(BF16)
        go[:, cols(h)] = g
        ql = (q[:, cols(h)].astype(F32) * lead_all[:, h : h + 1]).astype(BF16)
        own_x[h] = mm(ql, g, 0, 0)
        swap(own_x, sib_x, x_tx, x_rx, h).start()

    def local_back(h):
        g = go[:, cols(h)]
        w = (mm(g, v[:, cols(h)], 1, 1) * decay[h]).astype(BF16)
        out = mm(w, k[:, cols(h)]) + lead_all[:, h : h + 1] * mm(g, s_in[h], 1, 1)
        gq[:, cols(h)] = out.astype(BF16)
        part_k[:, cols(h)] = mm(w, q[:, cols(h)], 0, 0)
        part_v[:, cols(h)] = mm(fwd_w[h], g, 0, 0)

    for h in range(half):
        local_back(h)
    for h in range(heads):
        swap(own_x, sib_x, x_tx, x_rx, h).wait_recv()

    for j in range(half):
        h = half * c + j
        x0, x1 = pick(own_x, sib_x, h)
        l0, l1 = logs(h)
        pass_x[j] = x0 + jnp.exp(l0) * x1

        @pl.when(jnp.logical_not(has_next) & has_prev)
        def _():
            hop(pass_x, sgrad, f_tx, f_rx, j, -2).start()

    for h in range(half, heads):
        local_back(h)

    @pl.when(has_next)
    def _():
        for j in range(half):
            h = half * c + j
            hop(pass_x, sgrad, f_tx, f_rx, j, -2).wait_recv()
            give(sgrad, d_tx, d_rx, j).start()

            @pl.when(has_prev)
            def _():
                l0, l1 = logs(h)
                pass_x[j] = jnp.exp(l0 + l1) * sgrad[h] + pass_x[j]
                hop(pass_x, sgrad, f_tx, f_rx, j, -2).start()

        for j in range(half):
            take(sgrad, d_tx, d_rx, j).wait_recv()

    for h in range(heads):
        l_sib = sib_s[h, hd : hd + 1, :]
        f = sgrad[h]
        f = jnp.where(first, jnp.exp(l_sib) * f + sib_x[h], f).astype(BF16)
        tail = tail_all[:, h : h + 1]
        gk[:, cols(h)] = (part_k[:, cols(h)] + tail * mm(v[:, cols(h)], f, 1, 1)).astype(BF16)
        gv[:, cols(h)] = (part_v[:, cols(h)] + tail * mm(k[:, cols(h)], f)).astype(BF16)

    for h in range(heads):
        swap(own_s, sib_s, s_tx, s_rx, h).wait_send()
        swap(own_x, sib_x, x_tx, x_rx, h).wait_send()
    for d in range(1, nh):
        spread(d).wait_send()

    @pl.when(has_prev)
    def _():
        for j in range(half):
            give(state, c_tx, c_rx, j).wait_send()
            hop(pass_x, sgrad, f_tx, f_rx, j, -2).wait_send()

    @pl.when(has_next)
    def _():
        for j in range(half):
            give(sgrad, d_tx, d_rx, j).wait_send()
            hop(pass_s, state, e_tx, e_rx, j, 2).wait_send()


def on_device(queries, keys, values, log_decay, gain, grad_normed):
    toks, feats = queries.shape
    heads = log_decay.shape[1]
    hd = feats // heads
    half = heads // 2
    nz = lax.axis_size("ctx") // 2
    nh = lax.axis_size("head")
    vm = pl.BlockSpec(memory_space=pltpu.VMEM)
    dma = pltpu.SemaphoreType.DMA
    out = jax.ShapeDtypeStruct((toks, feats), BF16)
    others = max(nh - 1, 1)
    scratch = [
        pltpu.VMEM((heads, hd + 8, hd), F32),
        pltpu.VMEM((heads, hd + 8, hd), F32),
        pltpu.VMEM((heads, hd, hd), F32),
        pltpu.VMEM((half, hd, hd), F32),
        pltpu.VMEM((heads, hd, hd), F32),
        pltpu.VMEM((heads, hd, hd), F32),
        pltpu.VMEM((heads, hd, hd), F32),
        pltpu.VMEM((half, hd, hd), F32),
        pltpu.VMEM((8, toks), F32),
        pltpu.VMEM((others, 8, toks), F32),
        pltpu.VMEM((toks, feats), F32),
        pltpu.VMEM((toks, feats), BF16),
        pltpu.VMEM((heads, toks, toks), BF16),
        pltpu.VMEM((heads, toks, toks), F32),
        pltpu.VMEM((toks, feats), F32),
        pltpu.VMEM((toks, feats), F32),
        dma((heads,)), dma((heads,)),
        dma((half,)), dma((half,)),
        dma((half,)), dma((half,)),
        dma((others,)), dma((others,)),
        dma((heads,)), dma((heads,)),
        dma((half,)), dma((half,)),
        dma((half,)), dma((half,)),
    ]
    return pl.pallas_call(
        functools.partial(kernel, nz, nh, heads * hd * nh),
        out_shape=(out, out, out),
        in_specs=[vm] * 6,
        out_specs=(vm, vm, vm),
        scratch_shapes=scratch,
        compiler_params=pltpu.CompilerParams(
            collective_id=0, has_side_effects=True, vmem_limit_bytes=32 * 1024 * 1024
        ),
    )(queries, keys, values, log_decay, gain.reshape(1, feats), grad_normed)


def solution(mesh):
    in_specs = (
        P("ctx", "head"),
        P("ctx", "head"),
        P("ctx", "head"),
        P("ctx", "head"),
        P("head"),
        P("ctx", "head"),
    )
    out_specs = (P("ctx", "head"), P("ctx", "head"), P("ctx", "head"))
    return jax.shard_map(
        on_device, mesh=mesh, in_specs=in_specs, out_specs=out_specs, check_vma=False
    )
```

time: 107 us -> 46.4 us (0.43); the launches traced: 105 us -> 46.1 us
  waiting for transfers between devices: 48.3 us -> 0 us
  Pallas kernels: 0 us -> 38.7 us
  blocking collectives: 21.1 us -> 0 us
  between operations: 14.2 us -> 0.67 us
  other arithmetic: 9 us -> 0 us
  matrix products: 5.88 us -> 0 us
    all_gather x2 -> x0, waiting for transfers between devices: 48.2 us -> none  [prefix(): gathered = jax.tree.map(lambda a: lax.all_gather(a, axis), part)]
    pallas_call x0 -> x1, Pallas kernels: none -> 38.7 us  [on_device(): pl.pallas_call(functools.partial(kernel, nz, nh, heads * hd * nh), out_sh...]
    all_gather x1 -> x0, blocking collectives: 13.2 us -> none  [prefix(): gathered = jax.tree.map(lambda a: lax.all_gather(a, axis), part)]
    psum x1 -> x0, blocking collectives: 7.83 us -> none  [on_device(): sumsq, cross = lax.psum((local_sq, local_cross), 'head')]
    add x7 -> x0, other arithmetic: 7.43 us -> none  [combine_states(): jnp.exp(later[0])[:, None, None] * earlier[1] + later[1]]
    dot_general x12 -> x0, matrix products: 5.88 us -> none  [the longest x1 1.11 us: on_device(): own_grad = jnp.einsum('thi,thj->hij', q32 * lead, go32, precision=highest)]
    unnamed x12 -> x14, local copies, waits for them, and re-layouts: 4.73 us -> 6.73 us
    another operation x2 -> x0, other arithmetic: 1.24 us -> none
  transfers between devices with their start and end apart: 2 -> 0, of which waited for: 2 -> 0; matrix products, arithmetic and copies ran while one was open for 4% -> 0% of each run, Pallas kernels for 0% -> 0%
where the time goes in v1:
time: 46.4 us; the launch traced here: 46.1 us
  Pallas kernels  38.7 us (83%)
  local copies, waits for them, and re-layouts  6.73 us (15%)
  between operations  0.67 us (1%)
    pallas_call x1, Pallas kernels, on_device(): pl.pallas_call(functools.partial(kernel, nz, nh, heads * hd * nh), out_sh...  38.7 us
    unnamed x14, local copies, waits for them, and re-layouts  6.73 us

profile of v1, /device:TPU:1, one launch (start us, length us, event | category | flops | bytes accessed | tf_op | source)
XLA Modules:
  0.0 46.1 jit_solution(13744085359263603960)
XLA Ops:
  0.6 0.0 copy-start.4
  0.6 0.8 %copy.9.ld = f32[256,4]{1,0:T(8,128)S(1)} copy(f32[256,4]{0,1:T(4,128)} %param.9) | data formatting | bytes 8192 | tf_op args[3]
  1.5 0.0 copy-done.4
  1.5 0.0 copy-start
  1.5 0.9 %copy-done = bf16[256,512]{1,0:T(8,128)(2,1)S(1)} copy-done((bf16[256,512]{1,0:T(8,128)(2,1)S(1)}, bf16[256,512]{1,0:T(8,128)(2,1)}, u32[]{:S(2)}) %copy-start) | copy-done | bytes 262168
  2.4 0.0 copy-start.1
  2.4 0.9 %copy-done.1 = bf16[256,512]{1,0:T(8,128)(2,1)S(1)} copy-done((bf16[256,512]{1,0:T(8,128)(2,1)S(1)}, bf16[256,512]{1,0:T(8,128)(2,1)}, u32[]{:S(2)}) %copy-start.1) | copy-done | bytes 262168
  3.4 0.0 copy-start.2
  3.4 0.9 %copy-done.2 = bf16[256,512]{1,0:T(8,128)(2,1)S(1)} copy-done((bf16[256,512]{1,0:T(8,128)(2,1)S(1)}, bf16[256,512]{1,0:T(8,128)(2,1)}, u32[]{:S(2)}) %copy-start.2) | copy-done | bytes 262168
  4.3 0.0 copy-start.3
  4.3 0.9 %copy-done.3 = bf16[256,512]{1,0:T(8,128)(2,1)S(1)} copy-done((bf16[256,512]{1,0:T(8,128)(2,1)S(1)}, bf16[256,512]{1,0:T(8,128)(2,1)}, u32[]{:S(2)}) %copy-start.3) | copy-done | bytes 262168
  5.3 38.7 %shard_map.85 = (bf16[256,512]{1,0:T(8,128)(2,1)S(1)}, bf16[256,512]{1,0:T(8,128)(2,1)S(1)}, bf16[256,512]{1,0:T(8,128)(2,1)S(1)}) custom-call(bf16[256,512]{1,0:T(8,128)(2,1)S(1)} %copy-done, bf16[256,512]{1,0:T(8,128)(2,1)S(1)} %copy-done.1, bf16[256,512]{1,0:T(8,128)(2,1)S(1)} %copy-done.2, f32[256,4]{1,0:T(8,128)S(1)} %copy.9.ld, f32[1,512]{1,0:T(1,128)S(1)} %bitcast.1, ...), custom_call_target="tpu_custom_call" | custom-call | tf_op jit(solution)/shard_map/pallas_call | solution.py:312
  44.0 0.7 %copy.13 = bf16[256,512]{1,0:T(8,128)(2,1)} copy(bf16[256,512]{1,0:T(8,128)(2,1)S(1)} %get-tuple-element.6) | data formatting | bytes 524288
  44.7 0.7 %copy.14 = bf16[256,512]{1,0:T(8,128)(2,1)} copy(bf16[256,512]{1,0:T(8,128)(2,1)S(1)} %get-tuple-element.7) | data formatting | bytes 524288
  45.4 0.7 %copy.15 = bf16[256,512]{1,0:T(8,128)(2,1)} copy(bf16[256,512]{1,0:T(8,128)(2,1)S(1)} %get-tuple-element.8) | data formatting | bytes 524288
Async XLA Ops:
  0.6 0.8 %copy-start.4 = (f32[512]{0:T(512)S(1)}, f32[512]{0:T(512)}, u32[]{:S(2)}) copy-start(f32[512]{0:T(512)} %param.10) | copy-start | bytes 6148
  1.5 1.0 %copy-start = (bf16[256,512]{1,0:T(8,128)(2,1)S(1)}, bf16[256,512]{1,0:T(8,128)(2,1)}, u32[]{:S(2)}) copy-start(bf16[256,512]{1,0:T(8,128)(2,1)} %q.1) | copy-start | bytes 786436
  2.4 0.9 %copy-start.1 = (bf16[256,512]{1,0:T(8,128)(2,1)S(1)}, bf16[256,512]{1,0:T(8,128)(2,1)}, u32[]{:S(2)}) copy-start(bf16[256,512]{1,0:T(8,128)(2,1)} %k.1) | copy-start | bytes 786436
  3.4 0.9 %copy-start.2 = (bf16[256,512]{1,0:T(8,128)(2,1)S(1)}, bf16[256,512]{1,0:T(8,128)(2,1)}, u32[]{:S(2)}) copy-start(bf16[256,512]{1,0:T(8,128)(2,1)} %v.1) | copy-start | bytes 786436
  4.3 0.9 %copy-start.3 = (bf16[256,512]{1,0:T(8,128)(2,1)S(1)}, bf16[256,512]{1,0:T(8,128)(2,1)}, u32[]{:S(2)}) copy-start(bf16[256,512]{1,0:T(8,128)(2,1)} %dy.1) | copy-start | bytes 786436

commit v2 on v1

v2 whole, which is shorter than its diff:
```python
import functools

import jax
import jax.numpy as jnp
from jax import lax
from jax.experimental import pallas as pl
from jax.experimental.pallas import tpu as pltpu
from jax.sharding import PartitionSpec as P

F32 = jnp.float32
BF16 = jnp.bfloat16
MESH = pl.DeviceIdType.MESH
CUTS = 2


def mm(a, b, ca=1, cb=0):
    return lax.dot_general(a, b, (((ca,), (cb,)), ((), ())), preferred_element_type=F32)


def kernel(
    nz, nh, feats_all,
    q_h, k_h, v_h, ld_h, gain_h, dy_h,
    gq, gk, gv,
    q, k, v, ld, gain, dy,
    own_s, sib_s, state, pass_s, own_x, sib_x, sgrad, pass_x, red_tx, red_rx,
    attn, go, fwd_w, decay, part_k, part_v, gdy, lead, tail, ql_t, s_in, cum_s,
    in_sem, s_tx, s_rx, e_tx, e_rx, c_tx, c_rx, r_tx, r_rx, x_tx, x_rx, f_tx, f_rx, d_tx, d_rx,
):
    toks = q.shape[0]
    heads = ld.shape[0]
    hd = q.shape[1] // heads
    half = heads // 2
    rows = hd // CUTS
    me = lax.axis_index("ctx")
    grp = lax.axis_index("head")
    z = me // 2
    c = me % 2
    sib = me + 1 - 2 * c
    first = c == 0
    second = c == 1
    has_prev = z > 0
    has_next = z < nz - 1
    from_end = nz - 1 - z

    loads = [
        pltpu.make_async_copy(a, b, in_sem.at[i])
        for i, (a, b) in enumerate(
            ((ld_h, ld), (k_h, k), (v_h, v), (q_h, q), (dy_h, dy), (gain_h, gain))
        )
    ]
    for one in loads:
        one.start()

    def cols(h):
        if isinstance(h, int):
            return slice(h * hd, (h + 1) * hd)
        return pl.ds(pl.multiple_of(h * hd, hd), hd)

    def copy(src, dst, tx, rx, where):
        return pltpu.make_async_remote_copy(
            src_ref=src, dst_ref=dst, send_sem=tx, recv_sem=rx,
            device_id=where, device_id_type=MESH,
        )

    barrier = pltpu.get_barrier_semaphore()
    pl.semaphore_signal(barrier, inc=1, device_id={"ctx": sib}, device_id_type=MESH)
    for step in (2, 2 * nz - 2):
        pl.semaphore_signal(
            barrier, inc=1, device_id={"ctx": lax.rem(me + step, 2 * nz)}, device_id_type=MESH
        )
    for d in range(1, nh):
        pl.semaphore_signal(
            barrier, inc=1, device_id={"head": lax.rem(grp + d, nh)}, device_id_type=MESH
        )

    theirs = [half * (1 - c) + j for j in range(half)]
    mine = [half * c + j for j in range(half)]

    row = lax.broadcasted_iota(jnp.int32, (toks, toks), 0)
    col = lax.broadcasted_iota(jnp.int32, (toks, toks), 1)
    lower = row >= col
    upper = jnp.where(row <= col, 1.0, 0.0).astype(BF16)
    cum_s[...] = jnp.zeros_like(cum_s)
    loads[0].wait()
    logd = ld[...]
    high = logd.astype(BF16)
    rest = logd - high.astype(F32)
    mid = rest.astype(BF16)
    low = (rest - mid.astype(F32)).astype(BF16)
    cum_t = mm(high, upper) + mm(mid, upper) + mm(low, upper)
    cum_s[:heads, :] = cum_t
    cum = cum_s[...].T
    last = cum[toks - 1 : toks, :]
    lead_all = jnp.exp(cum)
    tail_all = jnp.exp(last - cum)
    for h in range(heads):
        tail[h] = jnp.broadcast_to(tail_all[:, h : h + 1], (toks, hd))
        log_h = jnp.broadcast_to(last[:, h : h + 1], (8, hd))
        own_s[h, hd:, :] = log_h
        own_x[h, hd:, :] = log_h
    loads[1].wait()
    loads[2].wait()

    def make_state(h):
        kt = (k[:, cols(h)].astype(F32) * tail[h]).astype(BF16)
        own_s[h, :hd, :] = mm(kt, v[:, cols(h)], 0, 0)

    def swap(src, dst, tx, rx, h, slot):
        return copy(src.at[h], dst.at[h], tx.at[slot], rx.at[slot], {"ctx": sib})

    for j in range(half):
        make_state(theirs[j])
        if j == 0:
            pl.semaphore_wait(barrier, 2 + nh)
        swap(own_s, sib_s, s_tx, s_rx, theirs[j], j).start()
    for j in range(half):
        make_state(mine[j])

        @pl.when(first)
        def _():
            swap(own_s, sib_s, s_tx, s_rx, mine[j], half + j).start()

    @pl.when(jnp.logical_not(has_prev))
    def _():
        state[...] = jnp.zeros_like(state)

    @pl.when(jnp.logical_not(has_next))
    def _():
        sgrad[...] = jnp.zeros_like(sgrad)

    def logs(h):
        a = own_s[h, hd : hd + 1, :]
        b = sib_s[h, hd : hd + 1, :]
        return jnp.where(first, a, b), jnp.where(first, b, a)

    def hop(buf, dst, tx, rx, j, i, step):
        part = pl.ds(i * rows, rows)
        n = j * CUTS + i
        return copy(
            buf.at[j, part], dst.at[mine[j], part], tx.at[n], rx.at[n], {"ctx": me + step}
        )

    def give(buf, tx, rx, j, i):
        part = pl.ds(i * rows, rows)
        n = j * CUTS + i
        return copy(buf.at[mine[j], part], buf.at[mine[j], part], tx.at[n], rx.at[n], {"ctx": sib})

    def take(buf, tx, rx, j, i):
        part = pl.ds(i * rows, rows)
        n = j * CUTS + i
        return copy(
            buf.at[theirs[j], part], buf.at[theirs[j], part], tx.at[n], rx.at[n], {"ctx": sib}
        )

    pieces = [(j, i) for j in range(half) for i in range(CUTS)]

    def chain(buf, dst, tx, rx, g_tx, g_rx, step, onward):
        both = []
        for j in range(half):
            l0, l1 = logs(mine[j])
            both.append(jnp.exp(l0 + l1))
        for j, i in pieces:
            part = pl.ds(i * rows, rows)
            hop(buf, dst, tx, rx, j, i, step).wait_recv()

            @pl.when(onward)
            def _():
                buf[j, part, :] = both[j] * dst[mine[j], part, :] + buf[j, part, :]
                hop(buf, dst, tx, rx, j, i, step).start()

            give(dst, g_tx, g_rx, j, i).start()

    def chain_fwd():
        chain(pass_s, state, e_tx, e_rx, c_tx, c_rx, 2, has_next)

    def chain_back():
        chain(pass_x, sgrad, f_tx, f_rx, d_tx, d_rx, -2, has_prev)

    for j in range(half):
        h = mine[j]
        swap(own_s, sib_s, s_tx, s_rx, h, j).wait_recv()
        l0, l1 = logs(h)
        a = own_s[h, :hd, :]
        b = sib_s[h, :hd, :]
        pass_s[j] = jnp.exp(l1) * jnp.where(first, a, b) + jnp.where(first, b, a)

        @pl.when(jnp.logical_not(has_prev) & has_next)
        def _():
            for i in range(CUTS):
                hop(pass_s, state, e_tx, e_rx, j, i, 2).start()

    @pl.when(z == 1)
    def _():
        chain_fwd()

    for one in loads[3:]:
        one.wait()
    for h in range(heads):
        diff = cum[:, h : h + 1] - cum_t[h : h + 1, :]
        dec = jnp.where(lower, jnp.exp(jnp.minimum(diff, 0.0)), 0.0)
        decay[h] = dec
        w = (mm(q[:, cols(h)], k[:, cols(h)], 1, 1) * dec).astype(BF16)
        fwd_w[h] = w
        attn[:, cols(h)] = mm(w, v[:, cols(h)])
        ahead = jnp.broadcast_to(lead_all[:, h : h + 1], (toks, hd))
        lead[h] = ahead
        ql_t[h] = (q[:, cols(h)].astype(F32) * ahead).astype(BF16).T
        gdy[:, cols(h)] = gain[:, cols(h)] * dy[:, cols(h)].astype(F32)

    @pl.when(z > 1)
    def _():
        chain_fwd()

    @pl.when(second)
    def _():
        for j in range(half):
            swap(own_s, sib_s, s_tx, s_rx, theirs[j], half + j).wait_recv()

    sq = jnp.zeros((toks, hd), F32)
    cr = jnp.zeros((toks, hd), F32)
    for n, h in enumerate(mine + theirs):
        if n >= half:
            @pl.when(has_prev)
            def _():
                for i in range(CUTS):
                    take(state, c_tx, c_rx, n - half, i).wait_recv()

        @pl.when(first)
        def _():
            s_in[h] = state[h].astype(BF16)

        @pl.when(second)
        def _():
            s_in[h] = (
                jnp.exp(sib_s[h, hd : hd + 1, :]) * state[h] + sib_s[h, :hd, :]
            ).astype(BF16)

        a = attn[:, cols(h)] + lead[h] * mm(q[:, cols(h)], s_in[h])
        attn[:, cols(h)] = a
        sq = sq + a * a
        cr = cr + gdy[:, cols(h)] * a
    lane = lax.broadcasted_iota(jnp.int32, (toks, 128), 1)
    sq = jnp.sum(sq, axis=1, keepdims=True)
    cr = jnp.sum(cr, axis=1, keepdims=True)
    both = jnp.where(lane == 0, sq, jnp.where(lane == 1, cr, 0.0)).T
    red_tx[...] = both[:8, :]

    def spread(d):
        return copy(
            red_tx, red_rx.at[d - 1], r_tx.at[d - 1], r_rx.at[d - 1],
            {"head": lax.rem(grp + d, nh)},
        )

    for d in range(1, nh):
        spread(d).start()
    total = red_tx[...]
    for d in range(1, nh):
        spread(d).wait_recv()
        total = total + red_rx[d - 1]
    rinv = 1.0 / jnp.sqrt(total[0:1, :] / feats_all + 1e-06)
    coef = total[1:2, :] * (rinv * rinv * rinv) / feats_all
    sub = lax.broadcasted_iota(jnp.int32, (128, toks), 0)
    scal = jnp.where(sub == 0, rinv, jnp.where(sub == 1, coef, 0.0)).T
    rinv_c = jnp.broadcast_to(scal[:, 0:1], (toks, hd))
    coef_c = jnp.broadcast_to(scal[:, 1:2], (toks, hd))

    def make_grad(h):
        g = (gdy[:, cols(h)] * rinv_c - attn[:, cols(h)] * coef_c).astype(BF16)
        go[:, cols(h)] = g
        own_x[h, :hd, :] = mm(ql_t[h], g)

    for j in range(half):
        make_grad(theirs[j])
        swap(own_x, sib_x, x_tx, x_rx, theirs[j], j).start()
    for j in range(half):
        make_grad(mine[j])

        @pl.when(second)
        def _():
            swap(own_x, sib_x, x_tx, x_rx, mine[j], half + j).start()

    for j in range(half):
        h = mine[j]
        swap(own_x, sib_x, x_tx, x_rx, h, j).wait_recv()
        l0, l1 = logs(h)
        a = own_x[h, :hd, :]
        b = sib_x[h, :hd, :]
        pass_x[j] = jnp.where(first, a, b) + jnp.exp(l0) * jnp.where(first, b, a)

        @pl.when(jnp.logical_not(has_next) & has_prev)
        def _():
            for i in range(CUTS):
                hop(pass_x, sgrad, f_tx, f_rx, j, i, -2).start()

    @pl.when(from_end == 1)
    def _():
        chain_back()

    for h in range(heads):
        g = go[:, cols(h)]
        w = (mm(g, v[:, cols(h)], 1, 1) * decay[h]).astype(BF16)
        out = mm(w, k[:, cols(h)]) + lead[h] * mm(g, s_in[h], 1, 1)
        gq[:, cols(h)] = out.astype(BF16)
        part_k[:, cols(h)] = mm(w, q[:, cols(h)], 0, 0)
        part_v[:, cols(h)] = mm(fwd_w[h], g, 0, 0)

    @pl.when(from_end > 1)
    def _():
        chain_back()

    @pl.when(first)
    def _():
        for j in range(half):
            swap(own_x, sib_x, x_tx, x_rx, theirs[j], half + j).wait_recv()

    for n, h in enumerate(mine + theirs):
        if n >= half:
            @pl.when(has_next)
            def _():
                for i in range(CUTS):
                    take(sgrad, d_tx, d_rx, n - half, i).wait_recv()

        @pl.when(second)
        def _():
            s_in[h] = sgrad[h].astype(BF16)

        @pl.when(first)
        def _():
            s_in[h] = (
                jnp.exp(sib_x[h, hd : hd + 1, :]) * sgrad[h] + sib_x[h, :hd, :]
            ).astype(BF16)

        f = s_in[h]
        gk[:, cols(h)] = (part_k[:, cols(h)] + tail[h] * mm(v[:, cols(h)], f, 1, 1)).astype(BF16)
        gv[:, cols(h)] = (part_v[:, cols(h)] + tail[h] * mm(k[:, cols(h)], f)).astype(BF16)

    for j in range(half):
        swap(own_s, sib_s, s_tx, s_rx, theirs[j], j).wait_send()
        swap(own_x, sib_x, x_tx, x_rx, theirs[j], j).wait_send()

        @pl.when(first)
        def _():
            swap(own_s, sib_s, s_tx, s_rx, mine[j], half + j).wait_send()

        @pl.when(second)
        def _():
            swap(own_x, sib_x, x_tx, x_rx, mine[j], half + j).wait_send()

    for d in range(1, nh):
        spread(d).wait_send()

    @pl.when(has_prev)
    def _():
        for j, i in pieces:
            give(state, c_tx, c_rx, j, i).wait_send()
            hop(pass_x, sgrad, f_tx, f_rx, j, i, -2).wait_send()

    @pl.when(has_next)
    def _():
        for j, i in pieces:
            give(sgrad, d_tx, d_rx, j, i).wait_send()
            hop(pass_s, state, e_tx, e_rx, j, i, 2).wait_send()


def on_device(queries, keys, values, log_decay, gain, grad_normed):
    toks, feats = queries.shape
    heads = log_decay.shape[1]
    hd = feats // heads
    half = heads // 2
    nz = lax.axis_size("ctx") // 2
    nh = lax.axis_size("head")
    vm = pl.BlockSpec(memory_space=pltpu.VMEM)
    hbm = pl.BlockSpec(memory_space=pltpu.HBM)
    dma = pltpu.SemaphoreType.DMA
    out = jax.ShapeDtypeStruct((toks, feats), BF16)
    others = max(nh - 1, 1)
    wide = pltpu.VMEM((toks, feats), BF16)
    wide32 = pltpu.VMEM((toks, feats), F32)
    per_head = pltpu.VMEM((heads, toks, hd), F32)
    tall = pltpu.VMEM((heads, hd + 8, hd), F32)
    full = pltpu.VMEM((heads, hd, hd), F32)
    part = pltpu.VMEM((half, hd, hd), F32)
    links = dma((half * CUTS,))
    scratch = [
        wide, wide, wide, pltpu.VMEM((heads, toks), F32), pltpu.VMEM((1, feats), F32), wide,
        tall, tall, full, part, tall, tall, full, part,
        pltpu.VMEM((8, toks), F32), pltpu.VMEM((others, 8, toks), F32),
        wide32, wide, pltpu.VMEM((heads, toks, toks), BF16),
        pltpu.VMEM((heads, toks, toks), F32), wide32, wide32, wide32,
        per_head, per_head, pltpu.VMEM((heads, hd, toks), BF16),
        pltpu.VMEM((heads, hd, hd), BF16), pltpu.VMEM((128, toks), F32),
        dma((6,)),
        dma((heads,)), dma((heads,)), links, links, links, links,
        dma((others,)), dma((others,)),
        dma((heads,)), dma((heads,)), links, links, links, links,
    ]
    return pl.pallas_call(
        functools.partial(kernel, nz, nh, heads * hd * nh),
        out_shape=(out, out, out),
        in_specs=[hbm] * 6,
        out_specs=(vm, vm, vm),
        scratch_shapes=scratch,
        compiler_params=pltpu.CompilerParams(
            collective_id=0, has_side_effects=True, vmem_limit_bytes=63 * 1024 * 1024
        ),
    )(queries, keys, values, log_decay.T, gain.reshape(1, feats), grad_normed)


def solution(mesh):
    in_specs = (
        P("ctx", "head"),
        P("ctx", "head"),
        P("ctx", "head"),
        P("ctx", "head"),
        P("head"),
        P("ctx", "head"),
    )
    out_specs = (P("ctx", "head"), P("ctx", "head"), P("ctx", "head"))
    return jax.shard_map(
        on_device, mesh=mesh, in_specs=in_specs, out_specs=out_specs, check_vma=False
    )
```

time: 46.4 us -> 40.9 us (0.88)
  local copies, waits for them, and re-layouts: 6.73 us -> 3.46 us
  Pallas kernels: 38.7 us -> 36.6 us
    unnamed x14 -> x7, local copies, waits for them, and re-layouts: 6.73 us -> 3.46 us
    pallas_call x1, Pallas kernels: 38.7 us -> 36.6 us  [on_device(): pl.pallas_call(functools.partial(kernel, nz, nh, heads * hd * nh), out_sh...]
where the time goes in v2:
time: 40.9 us; the launch traced here: 40.8 us
  Pallas kernels  36.6 us (89%)
  local copies, waits for them, and re-layouts  3.46 us (8%)
  between operations  0.65 us (2%)
    pallas_call x1, Pallas kernels, on_device(): pl.pallas_call(functools.partial(kernel, nz, nh, heads * hd * nh), out_sh...  36.6 us
    unnamed x7, local copies, waits for them, and re-layouts  3.46 us

profile of v2, /device:TPU:1, one launch (start us, length us, event | category | flops | bytes accessed | tf_op | source)
XLA Modules:
  0.0 40.8 jit_solution(17256773497806814476)
XLA Ops:
  0.6 36.6 %shard_map.85 = (bf16[256,512]{1,0:T(8,128)(2,1)}, bf16[256,512]{1,0:T(8,128)(2,1)}, bf16[256,512]{1,0:T(8,128)(2,1)}) custom-call(bf16[256,512]{1,0:T(8,128)(2,1)} %q_h.1, bf16[256,512]{1,0:T(8,128)(2,1)} %k_h.1, bf16[256,512]{1,0:T(8,128)(2,1)} %v_h.1, f32[4,256]{1,0:T(4,128)} %bitcast.2, f32[1,512]{1,0:T(1,128)} %bitcast.3, bf16[256,512]{1,0:T(8,128)(2,1)} %dy_h.1), custom_call_target="tpu_custom_call" | custom-call | tf_op jit(solution)/shard_map/pallas_call | solution.py:397
  37.3 0.0 copy-start.1
  37.3 1.7 %copy.12 = bf16[256,512]{1,0:T(8,128)(2,1)} copy(bf16[256,512]{1,0:T(8,128)(2,1)} %get-tuple-element.6) | data formatting | bytes 524288
  39.0 0.0 copy-done.1
  39.0 0.0 copy-start
  39.0 0.7 %copy.13 = bf16[256,512]{1,0:T(8,128)(2,1)} copy(bf16[256,512]{1,0:T(8,128)(2,1)S(1)} %copy-done.1) | data formatting | bytes 524288
  39.7 0.3 copy-done
  40.0 0.7 %copy.14 = bf16[256,512]{1,0:T(8,128)(2,1)} copy(bf16[256,512]{1,0:T(8,128)(2,1)S(1)} %copy-done) | data formatting | bytes 524288
Async XLA Ops:
  37.3 1.7 %copy-start.1 = (bf16[256,512]{1,0:T(8,128)(2,1)S(1)}, bf16[256,512]{1,0:T(8,128)(2,1)}, u32[]{:S(2)}) copy-start(bf16[256,512]{1,0:T(8,128)(2,1)} %get-tuple-element.7) | copy-start | bytes 786436
  39.0 1.0 %copy-start = (bf16[256,512]{1,0:T(8,128)(2,1)S(1)}, bf16[256,512]{1,0:T(8,128)(2,1)}, u32[]{:S(2)}) copy-start(bf16[256,512]{1,0:T(8,128)(2,1)} %get-tuple-element.8) | copy-start | bytes 786436

commit v3 on v2

--- a/solution.py
+++ b/solution.py
@@ -10,7 +10,7 @@
 F32 = jnp.float32
 BF16 = jnp.bfloat16
 MESH = pl.DeviceIdType.MESH
-CUTS = 2
+CUTS = 4
 
 
 def mm(a, b, ca=1, cb=0):
@@ -360,6 +360,17 @@
         for j, i in pieces:
             give(sgrad, d_tx, d_rx, j, i).wait_send()
             hop(pass_s, state, e_tx, e_rx, j, i, 2).wait_send()
+
+
+def hand_over(a, b, c, a_out, b_out, c_out, sem):
+    moves = [
+        pltpu.make_async_copy(src, dst, sem.at[i])
+        for i, (src, dst) in enumerate(((a, a_out), (b, b_out), (c, c_out)))
+    ]
+    for one in moves:
+        one.start()
+    for one in moves:
+        one.wait()
 
 
 def on_device(queries, keys, values, log_decay, gain, grad_normed):
@@ -394,16 +405,23 @@
         dma((others,)), dma((others,)),
         dma((heads,)), dma((heads,)), links, links, links, links,
     ]
-    return pl.pallas_call(
+    grads = pl.pallas_call(
         functools.partial(kernel, nz, nh, heads * hd * nh),
         out_shape=(out, out, out),
         in_specs=[hbm] * 6,
         out_specs=(vm, vm, vm),
         scratch_shapes=scratch,
         compiler_params=pltpu.CompilerParams(
-            collective_id=0, has_side_effects=True, vmem_limit_bytes=63 * 1024 * 1024
+            collective_id=0, has_side_effects=True, vmem_limit_bytes=62464 * 1024
         ),
     )(queries, keys, values, log_decay.T, gain.reshape(1, feats), grad_normed)
+    return pl.pallas_call(
+        hand_over,
+        out_shape=(out, out, out),
+        in_specs=[vm] * 3,
+        out_specs=(hbm, hbm, hbm),
+        scratch_shapes=[dma((3,))],
+    )(*grads)
 
 
 def solution(mesh):

time: 40.9 us -> 39 us (0.954)
  local copies, waits for them, and re-layouts: 3.46 us -> 0 us
  Pallas kernels: 36.6 us -> 38.2 us
    unnamed x7 -> x0, local copies, waits for them, and re-layouts: 3.46 us -> none
    pallas_call x0 -> x1, Pallas kernels: none -> 2.01 us  [on_device(): pl.pallas_call(hand_over, out_shape=(out, out, out), in_specs=[vm] * 3, o...]
    pallas_call x1, Pallas kernels: 36.6 us -> 36.2 us  [on_device(): pl.pallas_call(functools.partial(kernel, nz, nh, heads * hd * nh), out_sh...]
where the time goes in v3:
time: 39 us; the launch traced here: 38.8 us
  Pallas kernels  38.2 us (98%)
  between operations  0.64 us (2%)
    pallas_call x1, Pallas kernels, on_device(): pl.pallas_call(functools.partial(kernel, nz, nh, heads * hd * nh), out_sh...  36.2 us
    pallas_call x1, Pallas kernels, on_device(): pl.pallas_call(hand_over, out_shape=(out, out, out), in_specs=[vm] * 3, o...  2.01 us

profile of v3, /device:TPU:1, one launch (start us, length us, event | category | flops | bytes accessed | tf_op | source)
XLA Modules:
  0.0 38.8 jit_solution(14615650721056536564)
XLA Ops:
  0.6 36.2 %shard_map.85 = (bf16[256,512]{1,0:T(8,128)(2,1)}, bf16[256,512]{1,0:T(8,128)(2,1)}, bf16[256,512]{1,0:T(8,128)(2,1)}) custom-call(bf16[256,512]{1,0:T(8,128)(2,1)} %q_h.1, bf16[256,512]{1,0:T(8,128)(2,1)} %k_h.1, bf16[256,512]{1,0:T(8,128)(2,1)} %v_h.1, f32[4,256]{1,0:T(4,128)} %bitcast.2, f32[1,512]{1,0:T(1,128)} %bitcast.3, bf16[256,512]{1,0:T(8,128)(2,1)} %dy_h.1), custom_call_target="tpu_custom_call" | custom-call | tf_op jit(solution)/shard_map/pallas_call | solution.py:408
  36.8 2.0 %shard_map.86 = (bf16[256,512]{1,0:T(8,128)(2,1)}, bf16[256,512]{1,0:T(8,128)(2,1)}, bf16[256,512]{1,0:T(8,128)(2,1)}) custom-call(bf16[256,512]{1,0:T(8,128)(2,1)} %get-tuple-element.6.a, bf16[256,512]{1,0:T(8,128)(2,1)} %get-tuple-element.7.b, bf16[256,512]{1,0:T(8,128)(2,1)} %get-tuple-element.8.c), custom_call_target="tpu_custom_call" | custom-call | tf_op jit(solution)/shard_map/pallas_call | solution.py:418

commit v4 on v3

--- a/solution.py
+++ b/solution.py
@@ -20,7 +20,8 @@
 def kernel(
     nz, nh, feats_all,
     q_h, k_h, v_h, ld_h, gain_h, dy_h,
-    gq, gk, gv,
+    gq_h, gk_h, gv_h,
+    gq, gk, gv, out_sem,
     q, k, v, ld, gain, dy,
     own_s, sib_s, state, pass_s, own_x, sib_x, sgrad, pass_x, red_tx, red_rx,
     attn, go, fwd_w, decay, part_k, part_v, gdy, lead, tail, ql_t, s_in, cum_s,
@@ -303,6 +304,8 @@
         gq[:, cols(h)] = out.astype(BF16)
         part_k[:, cols(h)] = mm(w, q[:, cols(h)], 0, 0)
         part_v[:, cols(h)] = mm(fwd_w[h], g, 0, 0)
+    stores = [pltpu.make_async_copy(gq, gq_h, out_sem.at[0])]
+    stores[0].start()
 
     @pl.when(from_end > 1)
     def _():
@@ -333,6 +336,12 @@
         f = s_in[h]
         gk[:, cols(h)] = (part_k[:, cols(h)] + tail[h] * mm(v[:, cols(h)], f, 1, 1)).astype(BF16)
         gv[:, cols(h)] = (part_v[:, cols(h)] + tail[h] * mm(k[:, cols(h)], f)).astype(BF16)
+        for src, dst in ((gk, gk_h), (gv, gv_h)):
+            one = pltpu.make_async_copy(
+                src.at[:, cols(h)], dst.at[:, cols(h)], out_sem.at[len(stores)]
+            )
+            one.start()
+            stores.append(one)
 
     for j in range(half):
         swap(own_s, sib_s, s_tx, s_rx, theirs[j], j).wait_send()
@@ -346,6 +355,8 @@
         def _():
             swap(own_x, sib_x, x_tx, x_rx, mine[j], half + j).wait_send()
 
+    for one in stores:
+        one.wait()
     for d in range(1, nh):
         spread(d).wait_send()
 
@@ -362,14 +373,20 @@
             hop(pass_s, state, e_tx, e_rx, j, i, 2).wait_send()
 
 
-def hand_over(a, b, c, a_out, b_out, c_out, sem):
-    moves = [
-        pltpu.make_async_copy(src, dst, sem.at[i])
-        for i, (src, dst) in enumerate(((a, a_out), (b, b_out), (c, c_out)))
+def hand_over(a, b, c, a_out, b_out, c_out, held, in_sem, out_sem):
+    ins = [
+        pltpu.make_async_copy(src, held.at[i], in_sem.at[i]) for i, src in enumerate((a, b, c))
     ]
-    for one in moves:
+    outs = [
+        pltpu.make_async_copy(held.at[i], dst, out_sem.at[i])
+        for i, dst in enumerate((a_out, b_out, c_out))
+    ]
+    for one in ins:
         one.start()
-    for one in moves:
+    for got, put in zip(ins, outs):
+        got.wait()
+        put.start()
+    for one in outs:
         one.wait()
 
 
@@ -380,7 +397,6 @@
     half = heads // 2
     nz = lax.axis_size("ctx") // 2
     nh = lax.axis_size("head")
-    vm = pl.BlockSpec(memory_space=pltpu.VMEM)
     hbm = pl.BlockSpec(memory_space=pltpu.HBM)
     dma = pltpu.SemaphoreType.DMA
     out = jax.ShapeDtypeStruct((toks, feats), BF16)
@@ -393,6 +409,7 @@
     part = pltpu.VMEM((half, hd, hd), F32)
     links = dma((half * CUTS,))
     scratch = [
+        wide, wide, wide, dma((1 + 2 * heads,)),
         wide, wide, wide, pltpu.VMEM((heads, toks), F32), pltpu.VMEM((1, feats), F32), wide,
         tall, tall, full, part, tall, tall, full, part,
         pltpu.VMEM((8, toks), F32), pltpu.VMEM((others, 8, toks), F32),
@@ -409,7 +426,7 @@
         functools.partial(kernel, nz, nh, heads * hd * nh),
         out_shape=(out, out, out),
         in_specs=[hbm] * 6,
-        out_specs=(vm, vm, vm),
+        out_specs=(hbm, hbm, hbm),
         scratch_shapes=scratch,
         compiler_params=pltpu.CompilerParams(
             collective_id=0, has_side_effects=True, vmem_limit_bytes=62464 * 1024
@@ -418,9 +435,10 @@
     return pl.pallas_call(
         hand_over,
         out_shape=(out, out, out),
-        in_specs=[vm] * 3,
+        in_specs=[hbm] * 3,
         out_specs=(hbm, hbm, hbm),
-        scratch_shapes=[dma((3,))],
+        scratch_shapes=[pltpu.VMEM((3, toks, feats), BF16), dma((3,)), dma((3,))],
+        compiler_params=pltpu.CompilerParams(vmem_limit_bytes=62464 * 1024),
     )(*grads)
 
 

time: 39 us -> 38.7 us (level)
  no operation moved by 1% of the time
where the time goes in v4:
time: 38.7 us; the launch traced here: 38.5 us
  Pallas kernels  37.9 us (98%)
  between operations  0.64 us (2%)
    pallas_call x1, Pallas kernels, on_device(): pl.pallas_call(functools.partial(kernel, nz, nh, heads * hd * nh), out_sh...  36 us
    pallas_call x1, Pallas kernels, on_device(): pl.pallas_call(hand_over, out_shape=(out, out, out), in_specs=[hbm] * 3,...  1.88 us

profile of v4, /device:TPU:1, one launch (start us, length us, event | category | flops | bytes accessed | tf_op | source)
XLA Modules:
  0.0 38.5 jit_solution(5162899328926479333)
XLA Ops:
  0.6 36.0 %shard_map.85 = (bf16[256,512]{1,0:T(8,128)(2,1)}, bf16[256,512]{1,0:T(8,128)(2,1)}, bf16[256,512]{1,0:T(8,128)(2,1)}) custom-call(bf16[256,512]{1,0:T(8,128)(2,1)} %q_h.1, bf16[256,512]{1,0:T(8,128)(2,1)} %k_h.1, bf16[256,512]{1,0:T(8,128)(2,1)} %v_h.1, f32[4,256]{1,0:T(4,128)} %bitcast.2, f32[1,512]{1,0:T(1,128)} %bitcast.3, bf16[256,512]{1,0:T(8,128)(2,1)} %dy_h.1), custom_call_target="tpu_custom_call" | custom-call | tf_op jit(solution)/shard_map/pallas_call | solution.py:425
  36.6 1.9 %shard_map.86 = (bf16[256,512]{1,0:T(8,128)(2,1)}, bf16[256,512]{1,0:T(8,128)(2,1)}, bf16[256,512]{1,0:T(8,128)(2,1)}) custom-call(bf16[256,512]{1,0:T(8,128)(2,1)} %get-tuple-element.6.a, bf16[256,512]{1,0:T(8,128)(2,1)} %get-tuple-element.7.b, bf16[256,512]{1,0:T(8,128)(2,1)} %get-tuple-element.8.c), custom_call_target="tpu_custom_call" | custom-call | tf_op jit(solution)/shard_map/pallas_call | solution.py:435

commit v5 on v4

--- a/solution.py
+++ b/solution.py
@@ -374,13 +374,17 @@
 
 
 def hand_over(a, b, c, a_out, b_out, c_out, held, in_sem, out_sem):
-    ins = [
-        pltpu.make_async_copy(src, held.at[i], in_sem.at[i]) for i, src in enumerate((a, b, c))
-    ]
-    outs = [
-        pltpu.make_async_copy(held.at[i], dst, out_sem.at[i])
-        for i, dst in enumerate((a_out, b_out, c_out))
-    ]
+    rows = a.shape[0] // 2
+    ins, outs = [], []
+    for n, (src, dst) in enumerate(((a, a_out), (b, b_out), (c, c_out))):
+        for i in range(2):
+            part = pl.ds(i * rows, rows)
+            ins.append(
+                pltpu.make_async_copy(src.at[part], held.at[n, part], in_sem.at[2 * n + i])
+            )
+            outs.append(
+                pltpu.make_async_copy(held.at[n, part], dst.at[part], out_sem.at[2 * n + i])
+            )
     for one in ins:
         one.start()
     for got, put in zip(ins, outs):
@@ -437,7 +441,7 @@
         out_shape=(out, out, out),
         in_specs=[hbm] * 3,
         out_specs=(hbm, hbm, hbm),
-        scratch_shapes=[pltpu.VMEM((3, toks, feats), BF16), dma((3,)), dma((3,))],
+        scratch_shapes=[pltpu.VMEM((3, toks, feats), BF16), dma((6,)), dma((6,))],
         compiler_params=pltpu.CompilerParams(vmem_limit_bytes=62464 * 1024),
     )(*grads)
 

time: 38.7 us -> 38.8 us (level)
  no operation moved by 1% of the time
where the time goes in v5:
time: 38.8 us; the launch traced here: 38.6 us
  Pallas kernels  38 us (98%)
  between operations  0.64 us (2%)
    pallas_call x1, Pallas kernels, on_device(): pl.pallas_call(functools.partial(kernel, nz, nh, heads * hd * nh), out_sh...  36 us
    pallas_call x1, Pallas kernels, on_device(): pl.pallas_call(hand_over, out_shape=(out, out, out), in_specs=[hbm] * 3,...  1.97 us

profile of v5, /device:TPU:1, one launch (start us, length us, event | category | flops | bytes accessed | tf_op | source)
XLA Modules:
  0.0 38.6 jit_solution(10736280014166157976)
XLA Ops:
  0.6 36.0 %shard_map.85 = (bf16[256,512]{1,0:T(8,128)(2,1)}, bf16[256,512]{1,0:T(8,128)(2,1)}, bf16[256,512]{1,0:T(8,128)(2,1)}) custom-call(bf16[256,512]{1,0:T(8,128)(2,1)} %q_h.1, bf16[256,512]{1,0:T(8,128)(2,1)} %k_h.1, bf16[256,512]{1,0:T(8,128)(2,1)} %v_h.1, f32[4,256]{1,0:T(4,128)} %bitcast.2, f32[1,512]{1,0:T(1,128)} %bitcast.3, bf16[256,512]{1,0:T(8,128)(2,1)} %dy_h.1), custom_call_target="tpu_custom_call" | custom-call | tf_op jit(solution)/shard_map/pallas_call | solution.py:429
  36.6 2.0 %shard_map.86 = (bf16[256,512]{1,0:T(8,128)(2,1)}, bf16[256,512]{1,0:T(8,128)(2,1)}, bf16[256,512]{1,0:T(8,128)(2,1)}) custom-call(bf16[256,512]{1,0:T(8,128)(2,1)} %get-tuple-element.6.a, bf16[256,512]{1,0:T(8,128)(2,1)} %get-tuple-element.7.b, bf16[256,512]{1,0:T(8,128)(2,1)} %get-tuple-element.8.c), custom_call_target="tpu_custom_call" | custom-call | tf_op jit(solution)/shard_map/pallas_call | solution.py:439
